TPU v7x, 32 devices: a whole 2x2x4 slice. The times are simulated.
32 devices in a mesh: groups: 2 (over x), blk: 16 (over z, y, core).
Axes of the slice: x: 2, y: 2, z: 4, core: 2. Of those that a mesh axis runs over, the one named last changes fastest.
Arguments:
- queries: bfloat16 [32, 8192], P(('groups', 'blk')), parts along dimension 0, may hold values from -13 to 13
- cache_keys: bfloat16 [8192, 1024], P(('groups', 'blk')), parts along dimension 0, may hold values from -10 to 10
- cache_values: bfloat16 [8192, 1024], P(('groups', 'blk')), parts along dimension 0, may hold values from -5 to 5
- lengths: int32 [32], P(('groups', 'blk')), parts along dimension 0, may hold values from 1 to 256, as said below
- stretch_start: int32 [2], P('groups'), parts along dimension 0, may hold values from 2048 to 4080
- residual: float32 [32, 8192], P(('groups', 'blk')), parts along dimension 0, may hold values from -40 to 40
- out_weight: bfloat16 [8192, 8192], P('blk'), may hold values from -0.0625 to 0.0625
- norm_gain: float32 [8192], replicated, may hold values from 0.25 to 1.75
- gate_weight: bfloat16 [8192, 16384], P(None, 'blk'), may hold values from -0.0625 to 0.0625
- up_weight: bfloat16 [8192, 16384], P(None, 'blk'), may hold values from -0.0625 to 0.0625
- down_weight: bfloat16 [16384, 8192], P('blk'), may hold values from -0.046875 to 0.046875
Outputs:
- layer_out: float32 [32, 8192], P(('groups', 'blk')), parts along dimension 0
There are 2 independent parts, one for each index of `groups`. A program takes and returns all parts, laid end to end along the dimension named above; an argument that names none is the same for every part. Nothing has to cross between parts.
Inputs may be any that keep to these rules, and one draw needn't show every extreme that they name: `lengths`: each shard holds 1 to 256 live slots, and some shard is full.
All inputs are finite; a program needn't handle non-finite values.
Results may differ from a plain program's by a relative error of at most 0.0025.
Values may be sent and summed in bfloat16 or wider, within the bound.
A program may use at most 128 MiB of HBM per device.

v0:
```python
import jax
import jax.numpy as jnp
from jax import lax
from jax.sharding import PartitionSpec as P

QUERY_HEADS = 64
KV_HEADS = 8
HEAD_DIM = 128
NEG_FLOOR = -1e30
EPSILON = 1e-05


def body(
    queries,
    cache_keys,
    cache_values,
    lengths,
    stretch_start,
    residual,
    out_weight,
    norm_gain,
    gate_weight,
    up_weight,
    down_weight,
):
    group_size = QUERY_HEADS // KV_HEADS
    score_scale = HEAD_DIM ** (-0.5)
    span = group_size * HEAD_DIM
    all_queries = lax.all_gather(queries, "blk", axis=0, tiled=True)
    row_count = all_queries.shape[0]
    shard_len = cache_keys.shape[0]
    device = lax.axis_index("blk")
    slot_index = jnp.arange(shard_len, dtype=jnp.int32)
    position = device * shard_len + slot_index
    row_position = stretch_start[0] + jnp.arange(row_count, dtype=jnp.int32)
    visible = (slot_index[None, :] < lengths[0]) & (position[None, :] <= row_position[:, None])
    masked = visible[:, None, :]

    def head_step(head_index, state_in):
        numer_all, denom_all, peak_all = state_in
        q_block = lax.dynamic_slice_in_dim(all_queries, head_index * span, span, 1).reshape(
            row_count, group_size, HEAD_DIM
        )
        k_block = lax.dynamic_slice_in_dim(cache_keys, head_index * HEAD_DIM, HEAD_DIM, 1)
        v_block = lax.dynamic_slice_in_dim(cache_values, head_index * HEAD_DIM, HEAD_DIM, 1)
        scores = (
            jnp.einsum("rgd,kd->rgk", q_block, k_block, preferred_element_type=jnp.float32)
            * score_scale
        )
        local_max = jnp.max(jnp.where(masked, scores, NEG_FLOOR), axis=-1)
        weights = jnp.where(masked, jnp.exp(scores - local_max[:, :, None]), 0.0).astype(
            jnp.bfloat16
        )
        partial_out = jnp.einsum(
            "rgk,kd->rgd", weights, v_block, preferred_element_type=jnp.float32
        )
        partial_den = jnp.sum(weights, axis=-1, dtype=jnp.float32)
        numer_all = lax.dynamic_update_slice_in_dim(
            numer_all, partial_out.reshape(row_count, span), head_index * span, 1
        )
        denom_all = lax.dynamic_update_slice_in_dim(
            denom_all, partial_den, head_index * group_size, 1
        )
        peak_all = lax.dynamic_update_slice_in_dim(peak_all, local_max, head_index * group_size, 1)
        return (numer_all, denom_all, peak_all)

    start_state = (
        jnp.zeros((row_count, QUERY_HEADS * HEAD_DIM), jnp.float32),
        jnp.zeros((row_count, QUERY_HEADS), jnp.float32),
        jnp.zeros((row_count, QUERY_HEADS), jnp.float32),
    )
    numer_all, denom_all, peak_all = lax.fori_loop(0, KV_HEADS, head_step, start_state)
    global_max = lax.pmax(peak_all.astype(jnp.bfloat16), "blk").astype(peak_all.dtype)
    factor = jnp.exp(peak_all - global_max)
    scaled = (numer_all.reshape(row_count, QUERY_HEADS, HEAD_DIM) * factor[:, :, None]).reshape(
        row_count, QUERY_HEADS * HEAD_DIM
    )
    scaled_den = denom_all * factor
    numerator = lax.psum_scatter(scaled, "blk", scatter_dimension=1, tiled=True)
    denominator = lax.psum(scaled_den, "blk")
    col_count = numerator.shape[1]
    head_of = (device * col_count + jnp.arange(col_count, dtype=jnp.int32)) // HEAD_DIM
    head_pick = (jnp.arange(QUERY_HEADS, dtype=jnp.int32)[:, None] == head_of[None, :]).astype(
        jnp.float32
    )
    den_cols = jnp.dot(denominator, head_pick, precision=lax.Precision.HIGHEST)
    attn_cols = (numerator / den_cols).astype(jnp.bfloat16)
    picked = attn_cols
    attn_out = lax.psum_scatter(
        jnp.dot(picked, out_weight, preferred_element_type=jnp.float32),
        "blk",
        scatter_dimension=0,
        tiled=True,
    )
    mixed = residual + attn_out
    normed = (
        mixed * lax.rsqrt(jnp.mean(mixed * mixed, axis=-1, keepdims=True) + EPSILON) * norm_gain
    ).astype(jnp.bfloat16)
    row_piece = lax.all_gather(normed, "blk", axis=0, tiled=True)
    gate_term = jnp.dot(row_piece, gate_weight, preferred_element_type=jnp.float32)
    up_term = jnp.dot(row_piece, up_weight, preferred_element_type=jnp.float32)
    hidden_act = (jax.nn.silu(gate_term) * up_term).astype(jnp.bfloat16)
    picked = hidden_act
    ffn_out = lax.psum_scatter(
        jnp.dot(picked, down_weight, preferred_element_type=jnp.float32),
        "blk",
        scatter_dimension=0,
        tiled=True,
    )
    return mixed + ffn_out


def solution(mesh):
    in_specs = (
        P(("groups", "blk"), None),
        P(("groups", "blk"), None),
        P(("groups", "blk"), None),
        P(("groups", "blk")),
        P("groups"),
        P(("groups", "blk"), None),
        P("blk", None),
        P(),
        P(None, "blk"),
        P(None, "blk"),
        P("blk", None),
    )
    out_specs = P(("groups", "blk"), None)
    return jax.shard_map(body, mesh=mesh, in_specs=in_specs, out_specs=out_specs, check_vma=False)
```

profile of v0, /device:TPU:1, one launch (start us, length us, event | category | flops | bytes accessed | tf_op | source)
XLA Modules:
  0.0 380.7 jit_solution(13834208588220643452)
XLA Ops:
  6.5 24.8 %all-gather = bf16[16,1,8192]{2,1,0:T(2,128)(2,1)S(1)} all-gather(bf16[1,1,8192]{2,1,0:T(2,128)(2,1)} %bitcast.64), channel_id=1, replica_groups=mesh['groups'=2,'blk'=16] {'blk'}, dimensions={0}, use_global_device_ids=true | all-gather | bytes 278528 | tf_op jit(solution)/shard_map/all_gather | solution.py:29
  33.1 24.0 %while.18 = (s32[]{:T(128)}, f32[16,8192]{1,0:T(8,128)S(1)}, f32[16,64]{1,0:T(8,128)S(1)}, f32[16,64]{1,0:T(8,128)S(1)}, bf16[16,8192]{1,0:T(8,128)(2,1)S(1)}, /...) while((s32[]{:T(128)}, f32[16,8192]{1,0:T(8,128)S(1)}, ...), condition=%wide.region_3.4_spmd.clone, body=%wide.region_0.3_spmd.clone.sunk | while | flops 17145608 | bytes 906879 | solution.py:72
  33.2 1.1 select_reduce_fusion.2
  34.3 1.1 fusion.45
  36.1 1.1 select_reduce_fusion.2
  37.2 1.1 fusion.45
  39.2 1.1 select_reduce_fusion.2
  40.2 1.1 fusion.45
  42.2 1.1 select_reduce_fusion.2
  43.2 1.1 fusion.45
  45.2 1.1 select_reduce_fusion.2
  46.3 1.1 fusion.45
  48.2 1.1 select_reduce_fusion.2
  49.3 1.1 fusion.45
  51.2 1.1 select_reduce_fusion.2
  52.3 1.1 fusion.45
  54.2 1.1 select_reduce_fusion.2
  55.3 1.1 fusion.45
  57.1 29.0 %pmax.7 = bf16[16,64]{1,0:T(8,128)(2,1)S(1)} all-reduce(bf16[16,64]{1,0:T(8,128)(2,1)S(1)} %convert_element_type.30), channel_id=1, replica_groups=mesh['groups'=2,'blk'=16] {'blk'}, use_global_device_ids=true, to_apply=%region_4.5 | all-reduce | flops 1024 | bytes 4096 | tf_op jit(solution)/shard_map/pmax | solution.py:73
  86.3 1.1 bitcast_multiply_fusion
  87.6 30.3 %psum.7 = f32[16,64]{1,0:T(8,128)S(1)} all-reduce(f32[16,64]{1,0:T(8,128)S(1)} %get-tuple-element.196), channel_id=1, replica_groups=mesh['groups'=2,'blk'=16] {'blk'}, use_global_device_ids=true, to_apply=%region_6.7 | all-reduce | flops 1024 | bytes 8192 | tf_op jit(solution)/shard_map/psum | solution.py:80
  117.9 21.2 %reduce-scatter.2.cloned.1.call-done = f32[16,512]{1,0:T(8,128)} async-done(((f32[16,8192]{1,0:T(8,128)}), f32[16,512]{1,0:T(8,128)}) %reduce-scatter.2.cloned.1.call-update) | async-done | bytes 32784 | tf_op jit(solution)/shard_map/reduce_scatter | solution.py:79
  139.1 0.9 fusion.11
  140.0 5.4 %fusion.32 = f32[16,8192]{1,0:T(8,128)} fusion(bf16[16,512]{1,0:T(8,128)(2,1)S(1)} %fusion.11, bf16[512,8192]{1,0:T(8,128)(2,1)} %param.19), kind=kOutput, calls=%fused_computation.55 | convolution fusion | flops 134217728 | bytes 8929280 | tf_op jit(solution)/shard_map/dot_general | solution.py:90
  145.5 0.7 dynamic-slice
  146.2 91.0 %all-reduce.5.cloned.1.call-done = f32[16,8192]{1,0:T(8,128)} async-done(((f32[16,8192]{1,0:T(8,128)}), f32[16,8192]{1,0:T(8,128)}) %all-reduce.5.cloned.1.call-update) | async-done | bytes 524304
  237.2 2.3 multiply_reduce_fusion
  240.3 22.2 %all-gather.1 = bf16[16,1,8192]{2,1,0:T(2,128)(2,1)S(1)} all-gather(bf16[1,1,8192]{2,1,0:T(2,128)(2,1)S(1)} %convert_bitcast_fusion), channel_id=1, replica_groups=mesh['groups'=2,'blk'=16] {'blk'}, dimensions={0}, use_global_device_ids=true | all-gather | bytes 278528 | tf_op jit(solution)/shard_map/all_gather | solution.py:99
  262.5 8.0 %fusion.15 = f32[16,1024]{1,0:T(8,128)S(1)} fusion(bf16[8192,1024]{1,0:T(8,128)(2,1)} %param.21, bf16[16,1,8192]{2,1,0:T(2,128)(2,1)S(1)} %all-gather.1), kind=kOutput, calls=%fused_computation.23 | convolution fusion | flops 268435456 | bytes 17104896 | tf_op jit(solution)/shard_map/dot_general | solution.py:100
  270.5 13.7 %fusion.12 = f32[16,8192]{1,0:T(8,128)} fusion(bf16[1024,8192]{1,0:T(8,128)(2,1)} %param.23, bf16[8192,1024]{1,0:T(8,128)(2,1)} %param.22, bf16[16,1,8192]{2,1,0:T(2,128)(2,1)S(1)} %all-gather.1, f32[16,1024]{1,0:T(8,128)S(1)} %fusion.15), kind=kOutput, calls=%fused_computation.20 | convolution fusion | flops 536969216 | bytes 34406400 | tf_op jit(solution)/shard_map/dot_general | solution.py:105
  284.3 87.7 %all-reduce.7.cloned.1.call-done = f32[16,8192]{1,0:T(8,128)} async-done(((f32[16,8192]{1,0:T(8,128)}), f32[16,8192]{1,0:T(8,128)}) %all-reduce.7.cloned.1.call-update) | async-done | bytes 524304
  371.9 2.3 dynamic-slice_add_fusion
  (80 shorter events, 7.2 us)
Async XLA Ops:
  6.5 139.0 %copy-start.2 = (u32[32]{0:T(128)S(1)}, u32[32]{0:T(128)}, u32[]{:S(2)}) copy-start(u32[32]{0:T(128)} %constant.115) | copy-start | bytes 388
  6.5 230.7 %copy-start = (f32[1,8192]{1,0:T(1,128)S(1)}, f32[1,8192]{1,0:T(1,128)}, u32[]{:S(2)}) copy-start(f32[1,8192]{1,0:T(1,128)} %param.18) | copy-start | bytes 98308
  6.5 233.7 %copy-start.1 = (f32[8192]{0:T(1024)S(1)}, f32[8192]{0:T(1024)}, u32[]{:S(2)}) copy-start(f32[8192]{0:T(1024)} %param.20) | copy-start | bytes 98308
  6.5 132.6 %reduce-scatter.2.cloned.1.call-start = ((), (), s32[]{:S(2)}) async-start(), calls=%async_computation.1 | async-start | bytes 557056 | tf_op jit(solution)/shard_map/reduce_scatter | solution.py:79
  87.5 149.7 %all-reduce.5.cloned.1.call-start = ((), (), s32[]{:S(2)}) async-start(), calls=%async_computation.2 | async-start | bytes 1048576
  145.5 226.4 %all-reduce.7.cloned.1.call-start = ((), (), s32[]{:S(2)}) async-start(), calls=%async_computation.3 | async-start | bytes 1048576
Sparse Core Ops, SparseCore 0:
  87.6 51.4 reduce-scatter.1
  145.6 91.5 all-reduce.4
  284.4 87.4 all-reduce.6
where the time goes:
time: 382 us; the launch traced here: 381 us
  waiting for transfers between devices  200 us (52%)
  blocking collectives  106 us (28%)
  matrix products  45.2 us (12%)
  between operations  15.2 us (4%)
  other arithmetic  7.81 us (2%)
  local copies, waits for them, and re-layouts  5.68 us (1%)
    unnamed x5, waiting for transfers between devices  179 us
    psum x1, blocking collectives, body(): denominator = lax.psum(scaled_den, 'blk')  30.3 us
    pmax x1, blocking collectives, body(): lax.pmax(peak_all.astype(jnp.bfloat16), 'blk').astype(peak_all.dtype)  29 us
    all_gather x1, blocking collectives, body(): all_queries = lax.all_gather(queries, 'blk', axis=0, tiled=True)  24.8 us
    all_gather x1, blocking collectives, body(): row_piece = lax.all_gather(normed, 'blk', axis=0, tiled=True)  22.2 us
    reduce_scatter x1, waiting for transfers between devices, body(): numerator = lax.psum_scatter(scaled, 'blk', scatter_dimension=1, tiled=True)  21.2 us
    dot_general x1, matrix products, body(): jnp.dot(picked, down_weight, preferred_element_type=jnp.float32)  13.7 us
    dot_general x8, matrix products, head_step(): jnp.einsum('rgd,kd->rgk', q_block, k_block, preferred_element_type=jnp.fl...  8.7 us
  transfers between devices with their start and end apart: 3, of which 3 were waited for; matrix products, arithmetic and copies ran while one was open for 0% of the time, Pallas kernels for 0%

commit v1 on v0

--- a/solution.py
+++ b/solution.py
@@ -77,7 +77,8 @@
     )
     scaled_den = denom_all * factor
     numerator = lax.psum_scatter(scaled, "blk", scatter_dimension=1, tiled=True)
-    denominator = lax.psum(scaled_den, "blk")
+    begin_sums_all_for = lambda inp: jnp.sum(jax.lax.all_gather(inp, "blk"), axis=0)
+    denominator = begin_sums_all_for(scaled_den)
     col_count = numerator.shape[1]
     head_of = (device * col_count + jnp.arange(col_count, dtype=jnp.int32)) // HEAD_DIM
     head_pick = (jnp.arange(QUERY_HEADS, dtype=jnp.int32)[:, None] == head_of[None, :]).astype(

time: 382 us -> 382 us (level)
  waiting for transfers between devices: 200 us -> 212 us
  blocking collectives: 106 us -> 94.3 us
    psum x1 -> x0, blocking collectives: 30.3 us -> none  [body(): denominator = lax.psum(scaled_den, 'blk')]
    all_gather x0 -> x1, blocking collectives: none -> 18.3 us  [body(): jax.lax.all_gather(inp, 'blk')]
    reduce_scatter x1, waiting for transfers between devices: 21.2 us -> 33.2 us  [body(): numerator = lax.psum_scatter(scaled, 'blk', scatter_dimension=1, tiled=True)]
where the time goes in v1:
time: 382 us; the launch traced here: 381 us
  waiting for transfers between devices  212 us (55%)
  blocking collectives  94.3 us (25%)
  matrix products  45.2 us (12%)
  between operations  15.2 us (4%)
  other arithmetic  7.83 us (2%)
  local copies, waits for them, and re-layouts  5.68 us (1%)
    unnamed x5, waiting for transfers between devices  179 us
    reduce_scatter x1, waiting for transfers between devices, body(): numerator = lax.psum_scatter(scaled, 'blk', scatter_dimension=1, tiled=True)  33.2 us
    pmax x1, blocking collectives, body(): lax.pmax(peak_all.astype(jnp.bfloat16), 'blk').astype(peak_all.dtype)  29 us
    all_gather x1, blocking collectives, body(): all_queries = lax.all_gather(queries, 'blk', axis=0, tiled=True)  24.8 us
    all_gather x1, blocking collectives, body(): row_piece = lax.all_gather(normed, 'blk', axis=0, tiled=True)  22.2 us
    all_gather x1, blocking collectives, body(): jax.lax.all_gather(inp, 'blk')  18.3 us
    dot_general x1, matrix products, body(): jnp.dot(picked, down_weight, preferred_element_type=jnp.float32)  13.7 us
    dot_general x8, matrix products, head_step(): jnp.einsum('rgd,kd->rgk', q_block, k_block, preferred_element_type=jnp.fl...  8.7 us
  transfers between devices with their start and end apart: 3, of which 3 were waited for; matrix products, arithmetic and copies ran while one was open for 0% of the time, Pallas kernels for 0%

profile of v1, /device:TPU:1, one launch (start us, length us, event | category | flops | bytes accessed | tf_op | source)
XLA Modules:
  0.0 380.7 jit_solution(13739207883662288507)
XLA Ops:
  6.5 24.8 %all-gather.1 = bf16[16,1,8192]{2,1,0:T(2,128)(2,1)S(1)} all-gather(bf16[1,1,8192]{2,1,0:T(2,128)(2,1)} %bitcast.66), channel_id=1, replica_groups=mesh['groups'=2,'blk'=16] {'blk'}, dimensions={0}, use_global_device_ids=true | all-gather | bytes 278528 | tf_op jit(solution)/shard_map/all_gather | solution.py:29
  33.1 24.0 %while.18 = (s32[]{:T(128)}, f32[16,8192]{1,0:T(8,128)S(1)}, f32[16,64]{1,0:T(8,128)S(1)}, f32[16,64]{1,0:T(8,128)S(1)}, bf16[16,8192]{1,0:T(8,128)(2,1)S(1)}, /...) while((s32[]{:T(128)}, f32[16,8192]{1,0:T(8,128)S(1)}, ...), condition=%wide.region_3.4_spmd.clone, body=%wide.region_0.3_spmd.clone.sunk | while | flops 17145608 | bytes 906879 | solution.py:72
  33.2 1.1 select_reduce_fusion.2
  34.3 1.1 fusion.45
  36.1 1.1 select_reduce_fusion.2
  37.2 1.1 fusion.45
  39.2 1.1 select_reduce_fusion.2
  40.2 1.1 fusion.45
  42.2 1.1 select_reduce_fusion.2
  43.2 1.1 fusion.45
  45.2 1.1 select_reduce_fusion.2
  46.3 1.1 fusion.45
  48.2 1.1 select_reduce_fusion.2
  49.3 1.1 fusion.45
  51.2 1.1 select_reduce_fusion.2
  52.3 1.1 fusion.45
  54.2 1.1 select_reduce_fusion.2
  55.3 1.1 fusion.45
  57.1 29.0 %pmax.7 = bf16[16,64]{1,0:T(8,128)(2,1)S(1)} all-reduce(bf16[16,64]{1,0:T(8,128)(2,1)S(1)} %convert_element_type.30), channel_id=1, replica_groups=mesh['groups'=2,'blk'=16] {'blk'}, use_global_device_ids=true, to_apply=%region_4.5 | all-reduce | flops 1024 | bytes 4096 | tf_op jit(solution)/shard_map/pmax | solution.py:73
  86.3 1.1 bitcast_multiply_fusion
  87.6 18.3 %all-gather = f32[256,64]{1,0:T(8,128)S(1)} all-gather(f32[16,64]{1,0:T(8,128)S(1)} %get-tuple-element.196), channel_id=2, replica_groups=mesh['groups'=2,'blk'=16] {'blk'}, dimensions={0}, use_global_device_ids=true | all-gather | bytes 69632 | tf_op jit(solution)/shard_map/all_gather | solution.py:80
  105.9 33.2 %reduce-scatter.2.cloned.1.call-done = f32[16,512]{1,0:T(8,128)} async-done(((f32[16,8192]{1,0:T(8,128)}), f32[16,512]{1,0:T(8,128)}) %reduce-scatter.2.cloned.1.call-update) | async-done | bytes 32784 | tf_op jit(solution)/shard_map/reduce_scatter | solution.py:79
  139.1 0.9 fusion.11
  140.0 5.4 %fusion.32 = f32[16,8192]{1,0:T(8,128)} fusion(bf16[16,512]{1,0:T(8,128)(2,1)S(1)} %fusion.11, bf16[512,8192]{1,0:T(8,128)(2,1)} %param.19), kind=kOutput, calls=%fused_computation.55 | convolution fusion | flops 134217728 | bytes 8929280 | tf_op jit(solution)/shard_map/dot_general | solution.py:91
  145.5 0.7 dynamic-slice
  146.2 91.0 %all-reduce.5.cloned.1.call-done = f32[16,8192]{1,0:T(8,128)} async-done(((f32[16,8192]{1,0:T(8,128)}), f32[16,8192]{1,0:T(8,128)}) %all-reduce.5.cloned.1.call-update) | async-done | bytes 524304
  237.2 2.3 multiply_reduce_fusion
  240.3 22.2 %all-gather.2 = bf16[16,1,8192]{2,1,0:T(2,128)(2,1)S(1)} all-gather(bf16[1,1,8192]{2,1,0:T(2,128)(2,1)S(1)} %convert_bitcast_fusion), channel_id=1, replica_groups=mesh['groups'=2,'blk'=16] {'blk'}, dimensions={0}, use_global_device_ids=true | all-gather | bytes 278528 | tf_op jit(solution)/shard_map/all_gather | solution.py:100
  262.5 8.0 %fusion.15 = f32[16,1024]{1,0:T(8,128)S(1)} fusion(bf16[8192,1024]{1,0:T(8,128)(2,1)} %param.21, bf16[16,1,8192]{2,1,0:T(2,128)(2,1)S(1)} %all-gather.2), kind=kOutput, calls=%fused_computation.23 | convolution fusion | flops 268435456 | bytes 17104896 | tf_op jit(solution)/shard_map/dot_general | solution.py:101
  270.5 13.7 %fusion.12 = f32[16,8192]{1,0:T(8,128)} fusion(bf16[1024,8192]{1,0:T(8,128)(2,1)} %param.23, bf16[8192,1024]{1,0:T(8,128)(2,1)} %param.22, bf16[16,1,8192]{2,1,0:T(2,128)(2,1)S(1)} %all-gather.2, f32[16,1024]{1,0:T(8,128)S(1)} %fusion.15), kind=kOutput, calls=%fused_computation.20 | convolution fusion | flops 536969216 | bytes 34406400 | tf_op jit(solution)/shard_map/dot_general | solution.py:106
  284.3 87.7 %all-reduce.7.cloned.1.call-done = f32[16,8192]{1,0:T(8,128)} async-done(((f32[16,8192]{1,0:T(8,128)}), f32[16,8192]{1,0:T(8,128)}) %all-reduce.7.cloned.1.call-update) | async-done | bytes 524304
  371.9 2.3 dynamic-slice_add_fusion
  (81 shorter events, 7.2 us)
Async XLA Ops:
  6.5 139.0 %copy-start.2 = (u32[32]{0:T(128)S(1)}, u32[32]{0:T(128)}, u32[]{:S(2)}) copy-start(u32[32]{0:T(128)} %constant.115) | copy-start | bytes 388
  6.5 230.7 %copy-start = (f32[1,8192]{1,0:T(1,128)S(1)}, f32[1,8192]{1,0:T(1,128)}, u32[]{:S(2)}) copy-start(f32[1,8192]{1,0:T(1,128)} %param.18) | copy-start | bytes 98308
  6.5 233.7 %copy-start.1 = (f32[8192]{0:T(1024)S(1)}, f32[8192]{0:T(1024)}, u32[]{:S(2)}) copy-start(f32[8192]{0:T(1024)} %param.20) | copy-start | bytes 98308
  6.5 132.6 %reduce-scatter.2.cloned.1.call-start = ((), (), s32[]{:S(2)}) async-start(), calls=%async_computation.1 | async-start | bytes 557056 | tf_op jit(solution)/shard_map/reduce_scatter | solution.py:79
  87.5 149.7 %all-reduce.5.cloned.1.call-start = ((), (), s32[]{:S(2)}) async-start(), calls=%async_computation.2 | async-start | bytes 1048576
  145.5 226.4 %all-reduce.7.cloned.1.call-start = ((), (), s32[]{:S(2)}) async-start(), calls=%async_computation.3 | async-start | bytes 1048576
Sparse Core Ops, SparseCore 0:
  87.6 51.4 reduce-scatter.1
  145.6 91.5 all-reduce.4
  284.4 87.4 all-reduce.6
